TPU v7x, 32 devices: a whole 2x2x4 slice. The times are simulated.
32 devices in a mesh: groups: 2 (over y), gx: 8 (over z, x), gy: 2 (over core).
Axes of the slice: x: 2, y: 2, z: 4, core: 2. Of those that a mesh axis runs over, the one named last changes fastest.
Arguments:
- activations: bfloat16 [2, 256, 4096], P('gy', 'groups', 'gx'), parts along dimension 1, may hold values from -6 to 6
- gate_tiles: bfloat16 [256, 40, 128, 128], P('gx', 'gy'), may hold values from -0.09375 to 0.09375
- up_tiles: bfloat16 [256, 40, 128, 128], P('gx', 'gy'), may hold values from -0.09375 to 0.09375
- down_tiles: bfloat16 [256, 40, 128, 128], P('gx', 'gy'), may hold values from -0.046875 to 0.046875
- gate_slots: int32 [256, 40], P('gx', 'gy'), may hold values from -1 to 31, as said below
- up_slots: int32 [256, 40], P('gx', 'gy'), may hold values from -1 to 31, as said below
- down_slots: int32 [256, 40], P('gx', 'gy'), may hold values from -1 to 31, as said below
Outputs:
- mixed_out: bfloat16 [2, 256, 4096], P('gy', 'groups', 'gx'), parts along dimension 1
There are 2 independent parts, one for each index of `groups`. A program takes and returns all parts, laid end to end along the dimension named above; an argument that names none is the same for every part. Nothing has to cross between parts.
Inputs may be any that keep to these rules, and one draw needn't show every extreme that they name: `gate_slots`: in each block column and each half of the model width (the 20 slots of one half), the entries that are not -1 come first, are distinct, and number between 12 and 20; some list holds exactly 20. `up_slots`: as for gate_slots. `down_slots`: as for gate_slots.
All inputs are finite; a program needn't handle non-finite values.
Results may differ from a plain program's by a relative error of at most 0.005.
Values may be sent and summed in bfloat16 or wider, within the bound.
A program may use at most 256 MiB of HBM per device.

v0:
```python
import jax
import jax.numpy as jnp
from jax import lax
from jax.sharding import PartitionSpec as P


def mask_tiles(tile_set, slot_ids):
    return tile_set * (slot_ids >= 0).astype(tile_set.dtype)[:, :, None, None]


def project_dense(row_piece, tile_set, slot_ids):
    row_count = row_piece.shape[0]
    col_blocks, slot_count, tile_size, _ = tile_set.shape
    blocked = row_piece.reshape(row_count, -1, tile_size)
    chosen = jnp.take(blocked, jnp.maximum(slot_ids, 0).reshape(-1), axis=1)
    chosen = chosen.reshape(row_count, col_blocks, slot_count, tile_size)
    result = jnp.einsum("pfsk,fskn->pfn", chosen, tile_set, preferred_element_type=jnp.float32)
    return result.reshape(row_count, col_blocks * tile_size)


def spread_dense(hidden, tile_set, slot_ids, blocks):
    col_blocks, slot_count, tile_size, _ = tile_set.shape
    placing = (slot_ids[:, :, None] == jnp.arange(blocks)[None, None, :]).astype(jnp.bfloat16)
    placed = jnp.einsum("fsd,fskn->fkdn", placing, tile_set, preferred_element_type=jnp.float32)
    weight_block = placed.astype(jnp.bfloat16).reshape(col_blocks * tile_size, blocks * tile_size)
    return jnp.dot(hidden, weight_block, preferred_element_type=jnp.float32)


def body(activations, gate_tiles, up_tiles, down_tiles, gate_slots, up_slots, down_slots):
    members = lax.axis_size("gx")
    _, total_rows, column_count = activations.shape
    col_blocks, slot_count, tile_size, _ = gate_tiles.shape
    half_width = column_count * members
    blocks = half_width // tile_size
    gate_keep = mask_tiles(gate_tiles, gate_slots)
    up_keep = mask_tiles(up_tiles, up_slots)
    gathered = lax.all_gather(activations, "gx", axis=2, tiled=True)
    row_piece = gathered[0]
    gate_half = project_dense(row_piece, gate_keep, gate_slots)
    up_half = project_dense(row_piece, up_keep, up_slots)
    gate_full, up_full = lax.psum((gate_half, up_half), "gy")
    hidden = (jax.nn.silu(gate_full) * up_full).astype(jnp.bfloat16)
    partial_value = spread_dense(hidden, down_tiles, down_slots, blocks).reshape(
        total_rows, members, column_count
    )
    arrived = lax.all_to_all(partial_value, "gx", split_axis=1, concat_axis=1, tiled=True)
    mixed_out = jnp.sum(arrived, axis=1)
    return mixed_out.astype(jnp.bfloat16)[None, :, :]


def solution(mesh):
    placed = (
        P("gy", "groups", "gx"),
        P("gx", "gy", None, None),
        P("gx", "gy", None, None),
        P("gx", "gy", None, None),
        P("gx", "gy"),
        P("gx", "gy"),
        P("gx", "gy"),
    )
    return jax.shard_map(
        body, mesh=mesh, in_specs=placed, out_specs=P("gy", "groups", "gx"), check_vma=False
    )
```

profile of v0, /device:TPU:12, one launch (start us, length us, event | category | flops | bytes accessed | tf_op | source)
XLA Modules:
  0.0 323.4 jit_solution(7238560114511719330)
XLA Ops:
  6.5 0.0 all-gather.2.cloned.1.call-start
  6.5 1.7 copy.32
  8.2 0.0 all-gather.2.cloned.1.call-update
  8.2 0.0 all-reduce.3.cloned.1.call-start
  8.3 0.7 broadcast_maximum_fusion
  9.0 0.1 copy.37
  9.1 0.1 reshape.42
  9.2 0.7 compare_convert_fusion
  9.9 0.1 copy.36
  10.0 0.7 broadcast_maximum_fusion.1
  10.7 0.1 copy.31
  10.8 0.1 reshape.39
  10.9 0.7 compare_convert_fusion.1
  11.6 0.1 copy.30
  11.8 38.0 %all-gather.2.cloned.1.call-done = bf16[1,128,4096]{1,2,0:T(8,128)(2,1)} async-done(((bf16[1,128,512]{1,2,0:T(8,128)(2,1)}), bf16[1,128,4096]{1,2,0:T(8,128)(2,1)}) %all-gather.2.cloned.1.call-update) | async-done | bytes 1048592 | tf_op jit(solution)/shard_map/all_gather | solution.py:37
  49.8 1.6 copy.33
  51.4 16.5 %gather_fusion.1 = bf16[640,128,128]{2,1,0:T(8,128)(2,1)} fusion(bf16[128,32,128]{2,0,1:T(8,128)(2,1)S(1)} %copy.33, s32[1024]{0:T(1024)S(1)} %pad_clamp_fusion), kind=kCustom, calls=%fused_computation.1.clone | custom fusion | bytes 41945600 | tf_op jit(solution)/shard_map/jit(_take)/gather | solution.py:15
  68.0 18.1 %broadcast_select_fusion = bf16[640,128,128]{2,1,0:T(8,128)(2,1)} fusion(bf16[640,128,128]{2,1,0:T(8,128)(2,1)} %gather_fusion.1, pred[640]{0:T(1024)(128)(4,1)S(1)} %compare_and_fusion), kind=kLoop, calls=%fused_computation.9 | loop fusion | flops 10485760 | bytes 41943680 | tf_op jit(solution)/shard_map/jit(_take)/select_n | solution.py:15
  86.0 15.7 %fusion.2 = f32[32,128,128,1]{2,1,3,0:T(8,128)S(1)} fusion(bf16[128,32,20,128]{3,0,2,1:T(8,128)(2,1)} %bitcast.46, bf16[32,20,128,128]{3,2,1,0:T(8,128)(2,1)} %param.11, bf16[32,20]{1,0:T(8,128)(2,1)S(1)} %copy.36), kind=kOutput, calls=%fused_computation.5 | convolution fusion | flops 2694840320 | bytes 44041472 | tf_op jit(solution)/shard_map/pfsk,fskn->pfn/dot_general | solution.py:17
  101.7 1.8 copy.40
  103.6 16.5 %gather_fusion = bf16[640,128,128]{2,1,0:T(8,128)(2,1)} fusion(bf16[128,32,128]{2,0,1:T(8,128)(2,1)S(1)} %copy.33, s32[1024]{0:T(1024)S(1)} %pad_clamp_fusion.1), kind=kCustom, calls=%fused_computation.clone | custom fusion | bytes 41945600 | tf_op jit(solution)/shard_map/jit(_take)/gather | solution.py:15
  120.1 18.1 %broadcast_select_fusion.1 = bf16[640,128,128]{2,1,0:T(8,128)(2,1)} fusion(bf16[640,128,128]{2,1,0:T(8,128)(2,1)} %gather_fusion, pred[640]{0:T(1024)(128)(4,1)S(1)} %compare_and_fusion.1), kind=kLoop, calls=%fused_computation.10 | loop fusion | flops 10485760 | bytes 41943680 | tf_op jit(solution)/shard_map/jit(_take)/select_n | solution.py:15
  138.1 0.0 copy-start
  138.1 15.7 %fusion.4 = f32[32,128,128,1]{2,1,3,0:T(8,128)S(1)} fusion(bf16[128,32,20,128]{3,0,2,1:T(8,128)(2,1)} %bitcast.47, bf16[32,20,128,128]{3,2,1,0:T(8,128)(2,1)} %param.10, bf16[32,20]{1,0:T(8,128)(2,1)S(1)} %copy.30), kind=kOutput, calls=%fused_computation.7 | convolution fusion | flops 2694840320 | bytes 44041472 | tf_op jit(solution)/shard_map/pfsk,fskn->pfn/dot_general | solution.py:17
  153.8 2.0 copy.35
  155.9 0.0 all-reduce.3.cloned.1.call-update
  155.9 0.0 copy-done
  155.9 0.1 copy.41
  156.0 28.0 %fusion.6 = bf16[32,32,128,128]{3,1,2,0:T(8,128)(2,1)} fusion(bf16[32,20,128,128]{3,2,1,0:T(8,128)(2,1)} %param.12, s32[32,20]{1,0:T(8,128)S(1)} %copy.41), kind=kOutput, calls=%fused_computation.11 | convolution fusion | flops 687886336 | bytes 54528512 | tf_op jit(solution)/shard_map/fsd,fskn->fkdn/dot_general | solution.py:24
  183.9 22.7 %copy.55 = bf16[512,8,32,128]{3,1,2,0:T(8,128)(2,1)} copy(bf16[512,8,32,128]{3,2,1,0:T(8,128)(2,1)} %bitcast.44) | data formatting | bytes 67108864
  206.6 41.0 %copy.43 = bf16[4096,4096]{1,0:T(8,128)(2,1)} copy(bf16[4096,4096]{0,1:T(8,128)(2,1)} %bitcast.45) | data formatting | bytes 67108864 | tf_op jit(solution)/shard_map/dot_general | solution.py:26
  247.6 0.0 all-reduce.3.cloned.1.call-done
  247.6 16.8 %fusion.11 = f32[128,8,512]{2,0,1:T(8,128)S(1)} fusion(bf16[8,512,4096]{2,1,0:T(8,128)(2,1)} %bitcast.43, f32[128,4096]{1,0:T(8,128)} %get-tuple-element.6, f32[128,4096]{1,0:T(8,128)} %get-tuple-element.7), kind=kOutput, calls=%fused_computation.15 | convolution fusion | flops 4298113024 | bytes 39845888 | tf_op jit(solution)/shard_map/dot_general | solution.py:26
  264.5 51.2 %all_to_all.5 = f32[128,8,512]{2,0,1:T(8,128)S(1)} all-to-all(f32[128,8,512]{2,0,1:T(8,128)S(1)} %fusion.11), channel_id=1, replica_groups=mesh['groups'=2,'gx'=8,'gy'=2] {'gx'}, dimensions={1} | all-to-all | bytes 4194304 | tf_op jit(solution)/shard_map/all_to_all | solution.py:46
  315.7 0.9 reduce_sum.9
  (6 shorter events, 0.0 us)
Async XLA Ops:
  6.5 43.3 %all-gather.2.cloned.1.call-start = ((), (), s32[]{:S(2)}) async-start(), calls=%async_computation.1 | async-start | bytes 1179648 | tf_op jit(solution)/shard_map/all_gather | solution.py:37
  8.2 239.4 %all-reduce.3.cloned.1.call-start = ((), (), s32[]{:S(2)}) async-start(), calls=%async_computation.2 | async-start | bytes 8388608 | tf_op jit(solution)/shard_map/psum | solution.py:41
  138.1 17.8 %copy-start = (s32[32,20]{0,1:T(8,128)S(1)}, s32[32,20]{0,1:T(8,128)}, u32[]{:S(2)}) copy-start(s32[32,20]{0,1:T(8,128)} %param.15) | copy-start | bytes 7684
Sparse Core Ops, SparseCore 0:
  9.5 40.2 all-gather.1
  156.0 28.5 all-reduce.2
where the time goes:
time: 327 us; the launch traced here: 323 us
  local copies, waits for them, and re-layouts  104 us (32%)
  matrix products  76.2 us (23%)
  blocking collectives  51.2 us (16%)
  other arithmetic  39.9 us (12%)
  waiting for transfers between devices  38.1 us (12%)
  between operations  13.5 us (4%)
    all_to_all x1, blocking collectives, body(): lax.all_to_all(partial_value, 'gx', split_axis=1, concat_axis=1, tiled=True)  51.2 us
    dot_general x1, local copies, waits for them, and re-layouts, spread_dense(): return jnp.dot(hidden, weight_block, preferred_element_type=jnp.float32)  41 us
    all_gather x1, waiting for transfers between devices, body(): gathered = lax.all_gather(activations, 'gx', axis=2, tiled=True)  38 us
    select_n x4, other arithmetic, project_dense(): chosen = jnp.take(blocked, jnp.maximum(slot_ids, 0).reshape(-1), axis=1)  36.1 us
    gather x2, local copies, waits for them, and re-layouts, project_dense(): chosen = jnp.take(blocked, jnp.maximum(slot_ids, 0).reshape(-1), axis=1)  33 us
    dot_general x2, matrix products, project_dense(): jnp.einsum('pfsk,fskn->pfn', chosen, tile_set, preferred_element_type=jnp...  31.4 us
    dot_general x1, matrix products, spread_dense(): jnp.einsum('fsd,fskn->fkdn', placing, tile_set, preferred_element_type=jn...  28 us
    unnamed x5, local copies, waits for them, and re-layouts  24.4 us
  transfers between devices with their start and end apart: 2, of which 1 were waited for; matrix products, arithmetic and copies ran while one was open for 29% of the time, Pallas kernels for 0%

commit v1 on v0

--- a/solution.py
+++ b/solution.py
@@ -1,7 +1,17 @@
+import functools
+
 import jax
 import jax.numpy as jnp
 from jax import lax
+from jax.experimental import pallas as pl
+from jax.experimental.pallas import tpu as pltpu
 from jax.sharding import PartitionSpec as P
+
+MESH = pl.DeviceIdType.MESH
+LINE = 4
+GROUP = 4
+RING = 4
+DOWN_PARTS = 4
 
 
 def mask_tiles(tile_set, slot_ids):
@@ -26,12 +36,11 @@
     return jnp.dot(hidden, weight_block, preferred_element_type=jnp.float32)
 
 
-def body(activations, gate_tiles, up_tiles, down_tiles, gate_slots, up_slots, down_slots):
+def general_body(activations, gate_tiles, up_tiles, down_tiles, gate_slots, up_slots, down_slots):
     members = lax.axis_size("gx")
     _, total_rows, column_count = activations.shape
-    col_blocks, slot_count, tile_size, _ = gate_tiles.shape
     half_width = column_count * members
-    blocks = half_width // tile_size
+    blocks = half_width // gate_tiles.shape[2]
     gate_keep = mask_tiles(gate_tiles, gate_slots)
     up_keep = mask_tiles(up_tiles, up_slots)
     gathered = lax.all_gather(activations, "gx", axis=2, tiled=True)
@@ -48,6 +57,312 @@
     return mixed_out.astype(jnp.bfloat16)[None, :, :]
 
 
+def dot(a, b):
+    return jnp.dot(a, b, preferred_element_type=jnp.float32)
+
+
+def kernel(
+    gate_ids, up_ids, down_at, x_ref, gate_hbm, up_hbm, down_hbm, out_ref,
+    xg, wbuf, dbuf, sums, pair_out, pair_in, hid, yacc,
+    far_out, far_in, line_out, above_in, below_in,
+    wsem, dsem, pair_ssem, pair_rsem,
+    ag_xs, ag_xr, ag_us, ag_ds, ag_zr,
+    rs_xs, rs_xr, rs_zs, rs_ur, rs_dr,
+):
+    blk = xg.shape[1]
+    per = x_ref.shape[2] // blk
+    blocks = xg.shape[0] - 1
+    col_blocks, slots = gate_hbm.shape[0], gate_hbm.shape[1]
+    chunks = col_blocks // GROUP
+    tiles = down_hbm.shape[0]
+    dpart = tiles // DOWN_PARTS
+
+    me = lax.axis_index("gx")
+    z, xx = me // 2, me % 2
+    other = 2 * z + 1 - xx
+    core = 1 - lax.axis_index("gy")
+
+    def weight_copies(c):
+        b = c % RING
+        rows = pl.ds(c * GROUP, GROUP)
+        return (
+            pltpu.make_async_copy(gate_hbm.at[rows], wbuf.at[b, 0], wsem.at[b, 0]),
+            pltpu.make_async_copy(up_hbm.at[rows], wbuf.at[b, 1], wsem.at[b, 1]),
+        )
+
+    def down_copy(i):
+        rows = pl.ds(i * dpart, dpart)
+        return pltpu.make_async_copy(down_hbm.at[rows], dbuf.at[rows], dsem.at[i])
+
+    for c in range(min(RING, chunks)):
+        for copy in weight_copies(c):
+            copy.start()
+    for i in range(DOWN_PARTS):
+        down_copy(i).start()
+
+    barrier = pltpu.get_barrier_semaphore()
+    pl.semaphore_signal(barrier, inc=1, device_id={"gx": other}, device_id_type=MESH)
+    pl.semaphore_signal(barrier, inc=1, device_id={"gy": core}, device_id_type=MESH)
+
+    @pl.when(z > 0)
+    def _():
+        pl.semaphore_signal(barrier, inc=1, device_id={"gx": me - 2}, device_id_type=MESH)
+
+    @pl.when(z < LINE - 1)
+    def _():
+        pl.semaphore_signal(barrier, inc=1, device_id={"gx": me + 2}, device_id_type=MESH)
+
+    for b in range(per):
+        xg[me * per + b] = x_ref[0, :, b * blk : (b + 1) * blk]
+    xg[blocks] = jnp.zeros_like(xg[blocks])
+    dbuf[tiles] = jnp.zeros_like(dbuf[tiles])
+
+    pl.semaphore_wait(barrier, 2 + (z + LINE - 1) // LINE + (2 * LINE - 2 - z) // LINE)
+
+    def piece(zz, side):
+        return xg.at[pl.ds((2 * zz + side) * per, per)]
+
+    def line_copy(zz, send, to):
+        return pltpu.make_async_remote_copy(
+            src_ref=piece(zz, xx), dst_ref=piece(zz, xx), send_sem=send, recv_sem=ag_zr.at[zz],
+            device_id={"gx": to}, device_id_type=MESH,
+        )
+
+    def up_copy(s):
+        return line_copy(z - s, ag_us.at[s], me + 2)
+
+    def dn_copy(s):
+        return line_copy(z + s, ag_ds.at[s], me - 2)
+
+    def side_copy(zz, side):
+        return pltpu.make_async_remote_copy(
+            src_ref=piece(zz, side), dst_ref=piece(zz, side), send_sem=ag_xs.at[zz], recv_sem=ag_xr.at[zz],
+            device_id={"gx": other}, device_id_type=MESH,
+        )
+
+    @pl.when(z < LINE - 1)
+    def _():
+        up_copy(0).start()
+
+    @pl.when(z > 0)
+    def _():
+        dn_copy(0).start()
+
+    side_copy(z, xx).start()
+    for s in range(LINE - 1):
+        @pl.when(z - 1 - s >= 0)
+        def _():
+            line_copy(z - 1 - s, ag_us.at[s], me - 2).wait_recv()
+
+            @pl.when(z < LINE - 1)
+            def _():
+                up_copy(s + 1).start()
+
+            side_copy(z - 1 - s, xx).start()
+
+        @pl.when(z + 1 + s < LINE)
+        def _():
+            line_copy(z + 1 + s, ag_ds.at[s], me + 2).wait_recv()
+
+            @pl.when(z > 0)
+            def _():
+                dn_copy(s + 1).start()
+
+            side_copy(z + 1 + s, xx).start()
+
+    for zz in range(LINE):
+        side_copy(zz, 1 - xx).wait_recv()
+
+    def pair_copy(c):
+        return pltpu.make_async_remote_copy(
+            src_ref=pair_out.at[c], dst_ref=pair_in.at[c], send_sem=pair_ssem.at[c], recv_sem=pair_rsem.at[c],
+            device_id={"gy": core}, device_id_type=MESH,
+        )
+
+    def project(ids, b, which, j, f):
+        total = None
+        step = 4
+        for s0 in range(0, slots, step):
+            n = min(step, slots - s0)
+            left = jnp.concatenate([xg[ids[f, s0 + i]] for i in range(n)], axis=1)
+            right = wbuf[b, which, j, s0 : s0 + n].reshape(n * blk, blk)
+            term = dot(left, right)
+            total = term if total is None else total + term
+        return total
+
+    def activate(c):
+        pair_copy(c).wait_recv()
+        for j in range(GROUP):
+            cols = slice(j * blk, (j + 1) * blk)
+            gate = sums[c, 0, :, cols] + pair_in[c, 0, :, cols].astype(jnp.float32)
+            up = sums[c, 1, :, cols] + pair_in[c, 1, :, cols].astype(jnp.float32)
+            hid[c, :, cols] = (gate / (1.0 + jnp.exp(-gate)) * up).astype(hid.dtype)
+
+    @pl.loop(0, chunks)
+    def _(c):
+        b = c % RING
+        for copy in weight_copies(c):
+            copy.wait()
+        for j in range(GROUP):
+            cols = slice(j * blk, (j + 1) * blk)
+            f = c * GROUP + j
+            for which, ids in enumerate((gate_ids, up_ids)):
+                value = project(ids, b, which, j, f)
+                sums[c, which, :, cols] = value
+                pair_out[c, which, :, cols] = value.astype(pair_out.dtype)
+        pair_copy(c).start()
+
+        @pl.when(c + RING < chunks)
+        def _():
+            for copy in weight_copies(c + RING):
+                copy.start()
+
+        @pl.when(c > 0)
+        def _():
+            activate(c - 1)
+
+    for i in range(DOWN_PARTS):
+        down_copy(i).wait()
+    activate(chunks - 1)
+
+    def spread(dest):
+        for h in range(per // 2):
+            r = dest * per + 2 * h
+
+            def step(g, acc):
+                rows = []
+                for i in range(GROUP):
+                    f = g * GROUP + i
+                    rows.append(jnp.concatenate([dbuf[down_at[f, r]], dbuf[down_at[f, r + 1]]], axis=1))
+                return acc + dot(hid[g], jnp.concatenate(rows, axis=0))
+
+            yacc[:, 2 * h * blk : 2 * (h + 1) * blk] = lax.fori_loop(
+                0, chunks, step, jnp.zeros((xg.shape[1], 2 * blk), jnp.float32)
+            )
+
+    order = (3 * (1 - z // 2), (2 + 3 * z) % 5, 1 + z % 2, z)
+
+    def far_copy(zz):
+        return pltpu.make_async_remote_copy(
+            src_ref=far_out.at[zz], dst_ref=far_in.at[zz], send_sem=rs_xs.at[zz], recv_sem=rs_xr.at[zz],
+            device_id={"gx": other}, device_id_type=MESH,
+        )
+
+    def rise_copy(zz):
+        return pltpu.make_async_remote_copy(
+            src_ref=line_out.at[zz], dst_ref=below_in.at[zz], send_sem=rs_zs.at[zz], recv_sem=rs_ur.at[zz],
+            device_id={"gx": me + 2}, device_id_type=MESH,
+        )
+
+    def fall_copy(zz):
+        return pltpu.make_async_remote_copy(
+            src_ref=line_out.at[zz], dst_ref=above_in.at[zz], send_sem=rs_zs.at[zz], recv_sem=rs_dr.at[zz],
+            device_id={"gx": me - 2}, device_id_type=MESH,
+        )
+
+    for k in range(LINE):
+        zz = order[k]
+        spread(2 * zz + 1 - xx)
+        far_out[zz] = yacc[...].astype(far_out.dtype)
+        far_copy(zz).start()
+
+    for k in range(LINE):
+        zz = order[k]
+        spread(2 * zz + xx)
+        far_copy(zz).wait_recv()
+        yacc[...] += far_in[zz].astype(jnp.float32)
+
+        @pl.when((zz >= z) & (z > 0))
+        def _():
+            rise_copy(zz).wait_recv()
+            yacc[...] += below_in[zz].astype(jnp.float32)
+
+        @pl.when((zz <= z) & (z < LINE - 1))
+        def _():
+            fall_copy(zz).wait_recv()
+            yacc[...] += above_in[zz].astype(jnp.float32)
+
+        if k < LINE - 1:
+            line_out[zz] = yacc[...].astype(line_out.dtype)
+
+            @pl.when(zz > z)
+            def _():
+                rise_copy(zz).start()
+
+            @pl.when(zz < z)
+            def _():
+                fall_copy(zz).start()
+
+    out_ref[0] = yacc[...].astype(out_ref.dtype)
+
+    for c in range(chunks):
+        pair_copy(c).wait_send()
+    for zz in range(LINE):
+        side_copy(zz, xx).wait_send()
+        far_copy(zz).wait_send()
+    for s in range(LINE):
+        @pl.when((z < LINE - 1) & (z - s >= 0))
+        def _():
+            up_copy(s).wait_send()
+
+        @pl.when((z > 0) & (z + s < LINE))
+        def _():
+            dn_copy(s).wait_send()
+    for k in range(LINE - 1):
+        rise_copy(order[k]).wait_send()
+
+
+def line_body(activations, gate_tiles, up_tiles, down_tiles, gate_slots, up_slots, down_slots):
+    members = lax.axis_size("gx")
+    _, rows, columns = activations.shape
+    col_blocks, slots, blk, _ = gate_tiles.shape
+    blocks = columns * members // blk
+    tiles = col_blocks * slots
+    chunks = col_blocks // GROUP
+    gate_ids = jnp.where(gate_slots < 0, blocks, gate_slots)
+    up_ids = jnp.where(up_slots < 0, blocks, up_slots)
+    index = jnp.arange(tiles, dtype=jnp.int32).reshape(col_blocks, slots, 1) - tiles
+    match = down_slots[:, :, None] == jnp.arange(blocks, dtype=jnp.int32)[None, None, :]
+    down_at = tiles + jnp.sum(jnp.where(match, index, 0), axis=1)
+    bf16, f32 = jnp.bfloat16, jnp.float32
+    dma = pltpu.SemaphoreType.DMA
+    smem = pl.BlockSpec(memory_space=pltpu.SMEM)
+    vmem = pl.BlockSpec(memory_space=pltpu.VMEM)
+    hbm = pl.BlockSpec(memory_space=pltpu.HBM)
+    block = (LINE, rows, columns)
+    return pl.pallas_call(
+        kernel,
+        out_shape=jax.ShapeDtypeStruct(activations.shape, bf16),
+        in_specs=[smem, smem, smem, vmem, hbm, hbm, hbm],
+        out_specs=vmem,
+        scratch_shapes=[
+            pltpu.VMEM((blocks + 1, rows, blk), bf16),
+            pltpu.VMEM((RING, 2, GROUP, slots, blk, blk), bf16),
+            pltpu.VMEM((tiles + 1, blk, blk), bf16),
+            pltpu.VMEM((chunks, 2, rows, GROUP * blk), f32),
+            pltpu.VMEM((chunks, 2, rows, GROUP * blk), bf16),
+            pltpu.VMEM((chunks, 2, rows, GROUP * blk), bf16),
+            pltpu.VMEM((chunks, rows, GROUP * blk), bf16),
+            pltpu.VMEM((rows, columns), f32),
+            pltpu.VMEM(block, bf16),
+            pltpu.VMEM(block, bf16),
+            pltpu.VMEM(block, bf16),
+            pltpu.VMEM(block, bf16),
+            pltpu.VMEM(block, bf16),
+            dma((RING, 2)),
+            dma((DOWN_PARTS,)),
+            dma((chunks,)),
+            dma((chunks,)),
+        ] + [dma((LINE,))] * 10,
+        compiler_params=pltpu.CompilerParams(
+            collective_id=0, has_side_effects=True, vmem_limit_bytes=62 * 1024 * 1024
+        ),
+        cost_estimate=pl.CostEstimate(
+            flops=8 * rows * tiles * blk * blk, bytes_accessed=6 * tiles * blk * blk, transcendentals=0
+        ),
+    )(gate_ids, up_ids, down_at, activations, gate_tiles, up_tiles, down_tiles.reshape(tiles, blk, blk))
+
+
 def solution(mesh):
     placed = (
         P("gy", "groups", "gx"),
@@ -58,6 +373,14 @@
         P("gx", "gy"),
         P("gx", "gy"),
     )
+
+    def body(*args):
+        small = mesh.shape["gx"] == 2 * LINE and mesh.shape["gy"] == 2
+        _, rows, columns = args[0].shape
+        col_blocks, _, blk, _ = args[1].shape
+        fits = rows == blk and columns % (2 * blk) == 0 and col_blocks % GROUP == 0 and blk == 128
+        return line_body(*args) if small and fits else general_body(*args)
+
     return jax.shard_map(
         body, mesh=mesh, in_specs=placed, out_specs=P("gy", "groups", "gx"), check_vma=False
     )

time: 327 us -> 74.5 us (0.23)
  local copies, waits for them, and re-layouts: 104 us -> 3.13 us
  matrix products: 76.2 us -> 0 us
  Pallas kernels: 0 us -> 68.8 us
  blocking collectives: 51.2 us -> 0 us
  waiting for transfers between devices: 38.1 us -> 0 us
  other arithmetic: 39.9 us -> 2.16 us
  between operations: 13.5 us -> 0.02 us
    dot_general x4 -> x0, matrix products: 76.2 us -> none  [the longest x2 31.4 us: project_dense(): jnp.einsum('pfsk,fskn->pfn', chosen, tile_set, preferred_element_type=jnp...]
    pallas_call x0 -> x1, Pallas kernels: none -> 68.8 us  [line_body(): pl.pallas_call(kernel, out_shape=jax.ShapeDtypeStruct(activations.shape,...]
    all_to_all x1 -> x0, blocking collectives: 51.2 us -> none  [body(): lax.all_to_all(partial_value, 'gx', split_axis=1, concat_axis=1, tiled=True)]
    dot_general x1 -> x0, local copies, waits for them, and re-layouts: 41 us -> none  [spread_dense(): return jnp.dot(hidden, weight_block, preferred_element_type=jnp.float32)]
    all_gather x1 -> x0, waiting for transfers between devices: 38 us -> none  [body(): gathered = lax.all_gather(activations, 'gx', axis=2, tiled=True)]
    select_n x4 -> x1, other arithmetic: 36.1 us -> 0.61 us  [line_body(): up_ids = jnp.where(up_slots < 0, blocks, up_slots)]
    gather x2 -> x0, local copies, waits for them, and re-layouts: 33 us -> none  [project_dense(): chosen = jnp.take(blocked, jnp.maximum(slot_ids, 0).reshape(-1), axis=1)]
    unnamed x5 -> x3, local copies, waits for them, and re-layouts: 24.4 us -> 3.13 us
  transfers between devices with their start and end apart: 2 -> 0, of which waited for: 1 -> 0; matrix products, arithmetic and copies ran while one was open for 29% -> 0% of each run, Pallas kernels for 0% -> 0%
where the time goes in v1:
time: 74.5 us; the launch traced here: 74.1 us
  Pallas kernels  68.8 us (92%)
  local copies, waits for them, and re-layouts  3.13 us (4%)
  other arithmetic  2.16 us (3%)
    pallas_call x1, Pallas kernels, line_body(): pl.pallas_call(kernel, out_shape=jax.ShapeDtypeStruct(activations.shape,...  68.8 us
    unnamed x3, local copies, waits for them, and re-layouts  3.13 us

profile of v1, /device:TPU:12, one launch (start us, length us, event | category | flops | bytes accessed | tf_op | source)
XLA Modules:
  0.0 74.1 jit_solution(10940236550444794682)
XLA Ops:
  0.0 0.9 %select_reduce_fusion = s32[32,32]{1,0:T(8,128)S(1)} fusion(s32[32,20]{0,1:T(8,128)S(1)} %add_add_fusion, s32[32,20]{0,1:T(8,128)} %param.13), kind=kLoop, calls=%fused_computation | loop fusion | flops 60416 | bytes 9216 | tf_op jit(solution)/shard_map/reduce_sum | solution.py:326
  1.0 0.6 broadcast_add_fusion.down_at
  1.6 0.8 %copy.13 = s32[32,20]{1,0:T(8,128)S(1)} copy(s32[32,20]{0,1:T(8,128)} %param.11) | data formatting | bytes 5120 | tf_op args[4]
  2.3 0.8 %copy.15 = s32[32,20]{1,0:T(8,128)S(1)} copy(s32[32,20]{0,1:T(8,128)} %param.12) | data formatting | bytes 5120 | tf_op args[5]
  3.1 0.6 compare_select_fusion
  3.7 68.8 %shard_map.73 = bf16[1,128,512]{2,1,0:T(8,128)(2,1)} custom-call(s32[32,20]{1,0:T(8,128)} %get-tuple-element.6.gate_ids, s32[32,20]{1,0:T(8,128)} %get-tuple-element.5.up_ids, s32[32,32]{1,0:T(8,128)} %broadcast_add_fusion.down_at, bf16[1,128,512]{2,1,0:T(8,128)(2,1)} %x_ref.1, bf16[32,20,128,128]{3,2,1,0:T(8,128)(2,1)} %gate_hbm.1, ...), custom_call_target="tpu_custom_call" | custom-call | flops 10737418240 | bytes 62914560 | tf_op jit(solution)/shard_map/pallas_call | solution.py:333
  72.6 1.6 %copy.18 = bf16[1,128,512]{2,1,0:T(8,128)(2,1)} copy(bf16[1,128,512]{2,1,0:T(8,128)(2,1)} %shard_map.73) | data formatting | bytes 262144
  (1 shorter events, 0.0 us)

commit v2 on v1

--- a/solution.py
+++ b/solution.py
@@ -237,7 +237,7 @@
                 return acc + dot(hid[g], jnp.concatenate(rows, axis=0))
 
             yacc[:, 2 * h * blk : 2 * (h + 1) * blk] = lax.fori_loop(
-                0, chunks, step, jnp.zeros((xg.shape[1], 2 * blk), jnp.float32)
+                0, chunks, step, jnp.zeros((xg.shape[1], 2 * blk), jnp.float32), unroll=4
             )
 
     order = (3 * (1 - z // 2), (2 + 3 * z) % 5, 1 + z % 2, z)

time: 74.5 us -> 62.7 us (0.84)
  Pallas kernels: 68.8 us -> 57.1 us
    pallas_call x1, Pallas kernels: 68.8 us -> 57.1 us  [line_body(): pl.pallas_call(kernel, out_shape=jax.ShapeDtypeStruct(activations.shape,...]
where the time goes in v2:
time: 62.7 us; the launch traced here: 62.4 us
  Pallas kernels  57.1 us (91%)
  local copies, waits for them, and re-layouts  3.13 us (5%)
  other arithmetic  2.16 us (3%)
    pallas_call x1, Pallas kernels, line_body(): pl.pallas_call(kernel, out_shape=jax.ShapeDtypeStruct(activations.shape,...  57.1 us
    unnamed x3, local copies, waits for them, and re-layouts  3.13 us

profile of v2, /device:TPU:12, one launch (start us, length us, event | category | flops | bytes accessed | tf_op | source)
XLA Modules:
  0.0 62.4 jit_solution(3725281679415193772)
XLA Ops:
  0.0 0.9 %select_reduce_fusion = s32[32,32]{1,0:T(8,128)S(1)} fusion(s32[32,20]{0,1:T(8,128)S(1)} %add_add_fusion, s32[32,20]{0,1:T(8,128)} %param.13), kind=kLoop, calls=%fused_computation | loop fusion | flops 60416 | bytes 9216 | tf_op jit(solution)/shard_map/reduce_sum | solution.py:326
  1.0 0.6 broadcast_add_fusion.down_at
  1.6 0.8 %copy.13 = s32[32,20]{1,0:T(8,128)S(1)} copy(s32[32,20]{0,1:T(8,128)} %param.11) | data formatting | bytes 5120 | tf_op args[4]
  2.3 0.8 %copy.15 = s32[32,20]{1,0:T(8,128)S(1)} copy(s32[32,20]{0,1:T(8,128)} %param.12) | data formatting | bytes 5120 | tf_op args[5]
  3.1 0.6 compare_select_fusion
  3.7 57.1 %shard_map.73 = bf16[1,128,512]{2,1,0:T(8,128)(2,1)} custom-call(s32[32,20]{1,0:T(8,128)} %get-tuple-element.6.gate_ids, s32[32,20]{1,0:T(8,128)} %get-tuple-element.5.up_ids, s32[32,32]{1,0:T(8,128)} %broadcast_add_fusion.down_at, bf16[1,128,512]{2,1,0:T(8,128)(2,1)} %x_ref.1, bf16[32,20,128,128]{3,2,1,0:T(8,128)(2,1)} %gate_hbm.1, ...), custom_call_target="tpu_custom_call" | custom-call | flops 10737418240 | bytes 62914560 | tf_op jit(solution)/shard_map/pallas_call | solution.py:333
  60.8 1.6 %copy.18 = bf16[1,128,512]{2,1,0:T(8,128)(2,1)} copy(bf16[1,128,512]{2,1,0:T(8,128)(2,1)} %shard_map.73) | data formatting | bytes 262144
  (1 shorter events, 0.0 us)

commit v3 on v2

--- a/solution.py
+++ b/solution.py
@@ -237,7 +237,7 @@
                 return acc + dot(hid[g], jnp.concatenate(rows, axis=0))
 
             yacc[:, 2 * h * blk : 2 * (h + 1) * blk] = lax.fori_loop(
-                0, chunks, step, jnp.zeros((xg.shape[1], 2 * blk), jnp.float32), unroll=4
+                0, chunks, step, jnp.zeros((xg.shape[1], 2 * blk), jnp.float32), unroll=True
             )
 
     order = (3 * (1 - z // 2), (2 + 3 * z) % 5, 1 + z % 2, z)

time: 62.7 us -> 60.6 us (0.967)
  Pallas kernels: 57.1 us -> 55 us
    pallas_call x1, Pallas kernels: 57.1 us -> 55 us  [line_body(): pl.pallas_call(kernel, out_shape=jax.ShapeDtypeStruct(activations.shape,...]
where the time goes in v3:
time: 60.6 us; the launch traced here: 60.3 us
  Pallas kernels  55 us (91%)
  local copies, waits for them, and re-layouts  3.13 us (5%)
  other arithmetic  2.16 us (4%)
    pallas_call x1, Pallas kernels, line_body(): pl.pallas_call(kernel, out_shape=jax.ShapeDtypeStruct(activations.shape,...  55 us
    unnamed x3, local copies, waits for them, and re-layouts  3.13 us

profile of v3, /device:TPU:12, one launch (start us, length us, event | category | flops | bytes accessed | tf_op | source)
XLA Modules:
  0.0 60.3 jit_solution(1595041191322255617)
XLA Ops:
  0.0 0.9 %select_reduce_fusion = s32[32,32]{1,0:T(8,128)S(1)} fusion(s32[32,20]{0,1:T(8,128)S(1)} %add_add_fusion, s32[32,20]{0,1:T(8,128)} %param.13), kind=kLoop, calls=%fused_computation | loop fusion | flops 60416 | bytes 9216 | tf_op jit(solution)/shard_map/reduce_sum | solution.py:326
  1.0 0.6 broadcast_add_fusion.down_at
  1.6 0.8 %copy.13 = s32[32,20]{1,0:T(8,128)S(1)} copy(s32[32,20]{0,1:T(8,128)} %param.11) | data formatting | bytes 5120 | tf_op args[4]
  2.3 0.8 %copy.15 = s32[32,20]{1,0:T(8,128)S(1)} copy(s32[32,20]{0,1:T(8,128)} %param.12) | data formatting | bytes 5120 | tf_op args[5]
  3.1 0.6 %compare_select_fusion = (s32[32,20]{1,0:T(8,128)}, s32[32,20]{1,0:T(8,128)}) fusion(s32[32,20]{1,0:T(8,128)S(1)} %copy.15, s32[32,20]{1,0:T(8,128)S(1)} %copy.13), kind=kLoop, calls=%fused_computation.2 | loop fusion | flops 2560 | bytes 10240 | tf_op jit(solution)/shard_map/jit(_where)/select_n | solution.py:323
  3.7 55.0 %shard_map.73 = bf16[1,128,512]{2,1,0:T(8,128)(2,1)} custom-call(s32[32,20]{1,0:T(8,128)} %get-tuple-element.6.gate_ids, s32[32,20]{1,0:T(8,128)} %get-tuple-element.5.up_ids, s32[32,32]{1,0:T(8,128)} %broadcast_add_fusion.down_at, bf16[1,128,512]{2,1,0:T(8,128)(2,1)} %x_ref.1, bf16[32,20,128,128]{3,2,1,0:T(8,128)(2,1)} %gate_hbm.1, ...), custom_call_target="tpu_custom_call" | custom-call | flops 10737418240 | bytes 62914560 | tf_op jit(solution)/shard_map/pallas_call | solution.py:333
  58.7 1.6 %copy.18 = bf16[1,128,512]{2,1,0:T(8,128)(2,1)} copy(bf16[1,128,512]{2,1,0:T(8,128)(2,1)} %shard_map.73) | data formatting | bytes 262144
  (1 shorter events, 0.0 us)
